TPU v7x, 128 devices: a whole 4x4x4 slice. The times are simulated.
128 devices in a mesh: rows: 32 (over y_lo, z, x), cols: 4 (over y_hi, core).
Axes of the slice: x: 4, y: 4 (y_hi: 2, y_lo: 2; y = y_hi * 2 + y_lo), z: 4, core: 2. Of those that a mesh axis runs over, the one named last changes fastest.
Arguments:
- coords: float32 [2, 3, 262144], P(None, None, ('rows', 'cols')), may hold values from -6 to 6
- counts: bfloat16 [512, 8, 512, 512], P('rows', 'cols'), may hold values from 0 to 127, as said below
- tile_cols: int32 [512, 8], P('rows', 'cols'), may hold values from -1 to 511, as said below
- exponents: int32 [512, 8], P('rows', 'cols'), may hold values from 4 to 7
- chrom_starts: int32 [24], replicated, may hold values from 0 to 261632, as said below
Outputs:
- gradient: float32 [2, 3, 262144], P(None, None, ('rows', 'cols'))
Inputs may be any that keep to these rules, and one draw needn't show every extreme that they name: `counts`: whole numbers. `tile_cols`: the live slots of one row tile and column group come first and name distinct tiles of that group; the group that holds the row tile's own index has all 2 slots live and names that index. `chrom_starts`: strictly rising, first entry 0, last entry 261632.
All inputs are finite; a program needn't handle non-finite values.
Results may differ from a plain program's by a relative error of at most 0.0003.
Values sent between devices are 32-bit elements; how exact they have to be, the bound alone decides.
No kernel may reach another device: no remote copies, remote signals or barrier semaphores. Data moves between devices by JAX's collectives and lax.ppermute only.
A program may use at most 448 MiB of HBM per device.

v0:
```python
import jax
import jax.numpy as jnp
from jax import lax
from jax.sharding import PartitionSpec as P

BETA_SAME = 8.0
BETA_OTHER = 2.0
REPULSE = 24.0


def chrom_of(first_bin, width, starts):
    bin_ids = first_bin + lax.iota(jnp.int32, width)
    return jnp.sum((bin_ids[:, None] >= starts[None, :]).astype(jnp.int32), axis=1) - 1


def tile_terms(row_pos, col_pos, tile_counts, exponent, row_chrom, col_chrom, is_live):
    factor = jnp.exp2(-exponent.astype(jnp.float32))
    observed = tile_counts.astype(jnp.float32) * factor
    tile_size = tile_counts.shape[0]
    distance = jnp.zeros((row_pos.shape[0], tile_size, tile_size), jnp.float32)
    for component in range(3):
        offset = row_pos[:, component, :, None] - col_pos[:, component, None, :]
        distance = distance + offset * offset
    inverse = 1.0 / (1.0 + distance)
    affinity = jnp.where(row_chrom[:, None] == col_chrom[None, :], BETA_SAME, BETA_OTHER)
    expected = affinity * inverse * jnp.sqrt(inverse)
    slopes = (
        2.0
        * (-1.5 * (expected - observed) * inverse - 2.0 * REPULSE * inverse * inverse * inverse)
        / tile_size
    )
    slopes = slopes * is_live
    row_grad = row_pos * jnp.sum(slopes, axis=2)[:, None, :] - jnp.einsum(
        "tij,tcj->tci", slopes, col_pos, precision=lax.Precision.HIGHEST
    )
    col_grad = col_pos * jnp.sum(slopes, axis=1)[:, None, :] - jnp.einsum(
        "tij,tci->tcj", slopes, row_pos, precision=lax.Precision.HIGHEST
    )
    return (row_grad, col_grad)


def body(coords, counts, tile_cols, exponents, chrom_starts):
    row_tiles = counts.shape[0]
    slot_count = counts.shape[1]
    tile_size = counts.shape[2]
    piece_tiles = coords.shape[2] // tile_size
    col_count = lax.axis_size("cols")
    row_first = lax.axis_index("rows") * (row_tiles * tile_size)
    tile_total = row_tiles * slot_count
    turn_count = min(16, tile_total)
    per_turn = tile_total // turn_count
    rows_all = (jnp.arange(tile_total, dtype=jnp.int32) // slot_count).reshape(turn_count, per_turn)
    tile_map = jax.vmap(tile_terms, in_axes=(2, 2, 0, 0, 0, 0, 0), out_axes=(2, 2))
    chroms = jax.vmap(chrom_of, in_axes=(0, None, None))
    row_pos = lax.all_gather(coords, "cols", axis=2, tiled=True)
    col_pos = lax.all_gather(coords, "rows", axis=2, tiled=True)
    trial_count = row_pos.shape[0]
    row_blocks = row_pos.reshape(trial_count, 3, row_tiles, tile_size)
    col_blocks = col_pos.reshape(trial_count, 3, col_pos.shape[2] // tile_size, tile_size)

    def tile_step(totals, inputs):
        row_part, col_part = totals
        tile_counts, columns, exponent_row, tile_rows = inputs
        is_live = (columns >= 0).astype(jnp.float32)
        safe_cols = jnp.maximum(columns, 0)
        local_cols = safe_cols // (piece_tiles * col_count) * piece_tiles + safe_cols % piece_tiles
        row_tile = row_blocks[:, :, tile_rows]
        col_tile = col_blocks[:, :, local_cols]
        row_chrom = chroms(row_first + tile_rows * tile_size, tile_size, chrom_starts)
        col_chrom = chroms(safe_cols * tile_size, tile_size, chrom_starts)
        row_grad, col_grad = tile_map(
            row_tile, col_tile, tile_counts, exponent_row, row_chrom, col_chrom, is_live
        )
        row_part = row_part.at[:, :, tile_rows].add(row_grad)
        col_part = col_part.at[:, :, local_cols].add(col_grad)
        return ((row_part, col_part), None)

    initial = (jnp.zeros(row_blocks.shape, jnp.float32), jnp.zeros(col_blocks.shape, jnp.float32))
    (row_part, col_part), _ = lax.scan(tile_step, initial, (counts, tile_cols, exponents, rows_all))
    row_part, col_part = (row_part.reshape(row_pos.shape), col_part.reshape(col_pos.shape))
    col_grad = lax.psum_scatter(col_part, "rows", scatter_dimension=2, tiled=True)
    row_grad = lax.psum_scatter(row_part, "cols", scatter_dimension=2, tiled=True)
    return row_grad + col_grad


def solution(mesh):
    placed = (
        P(None, None, ("rows", "cols")),
        P("rows", "cols", None, None),
        P("rows", "cols"),
        P("rows", "cols"),
        P(),
    )
    return jax.shard_map(
        body, mesh=mesh, in_specs=placed, out_specs=P(None, None, ("rows", "cols")), check_vma=False
    )
```

profile of v0, /device:TPU:0, one launch (start us, length us, event | category | flops | bytes accessed | tf_op | source)
XLA Modules:
  0.0 1173.7 jit_solution(3777700436996368370)
XLA Ops:
  8.8 7.4 all_gather.6
  16.2 147.7 %all-gather.2.cloned.1.call-done = f32[2,3,65536]{2,0,1:T(2,128)} async-done(((f32[2,3,2048]{2,0,1:T(2,128)}), f32[2,3,65536]{2,0,1:T(2,128)}) %all-gather.2.cloned.1.call-update) | async-done | bytes 1572880 | tf_op jit(solution)/shard_map/all_gather | solution.py:56
  164.4 397.6 %while.15 = (s32[]{:T(128)}, f32[2,3,16,512]{3,0,2,1:T(2,128)S(1)}, f32[2,3,128,512]{3,0,2,1:T(2,128)S(1)}, s32[16,2]{1,0:T(8,128)S(1)}, f32[2,3,16,512]{3,0,2,1...) while((s32[]{:T(128)}, f32[2,3,16,512]{3,0,2,1:T(2,128)S(1)}, ...), condition=%wide.region_7.8_spmd, body=%wide.region_0.7_spmd.sunk | while | flops 142790720 | bytes 18850224 | solution.py:79
  165.4 2.0 gather_fusion
  170.0 4.7 fusion.31
  174.7 6.0 fusion.33
  180.7 7.1 fusion.32
  194.8 4.7 fusion.31
  199.6 6.0 fusion.33
  205.6 7.1 fusion.32
  215.1 2.0 gather_fusion
  219.7 4.7 fusion.31
  224.4 6.0 fusion.33
  230.4 7.1 fusion.32
  240.0 2.0 gather_fusion
  244.5 4.7 fusion.31
  249.3 6.0 fusion.33
  255.3 7.1 fusion.32
  269.4 4.7 fusion.31
  274.1 6.0 fusion.33
  280.1 7.1 fusion.32
  289.7 2.0 gather_fusion
  294.2 4.7 fusion.31
  299.0 6.0 fusion.33
  305.0 7.1 fusion.32
  319.1 4.7 fusion.31
  323.8 6.0 fusion.33
  329.8 7.1 fusion.32
  343.9 4.7 fusion.31
  348.7 6.0 fusion.33
  354.7 7.1 fusion.32
  368.8 4.7 fusion.31
  373.5 6.0 fusion.33
  379.5 7.1 fusion.32
  393.6 4.7 fusion.31
  398.4 6.0 fusion.33
  404.4 7.1 fusion.32
  418.5 4.7 fusion.31
  423.2 6.0 fusion.33
  429.2 7.1 fusion.32
  443.3 4.7 fusion.31
  448.1 6.0 fusion.33
  454.1 7.1 fusion.32
  468.2 4.7 fusion.31
  472.9 6.0 fusion.33
  478.9 7.1 fusion.32
  493.0 4.7 fusion.31
  497.8 6.0 fusion.33
  503.8 7.1 fusion.32
  517.9 4.7 fusion.31
  522.6 6.0 fusion.33
  528.6 7.1 fusion.32
  542.7 4.7 fusion.31
  547.5 6.0 fusion.33
  553.5 7.1 fusion.32
  562.0 10.7 copy.44
  572.7 16.6 %reshape.307 = f32[8192,6]{1,0:T(8,128)} reshape(f32[8192,3,2]{2,1,0:T(4,128)} %bitcast.153) | data formatting | bytes 393216
  589.5 78.7 %copy.46 = f32[2,3,65536]{0,1,2:T(4,128)} copy(f32[2,3,65536]{2,0,1:T(2,128)S(1)} %bitcast.156) | data formatting | bytes 3145728
  668.2 124.8 %reshape.309 = f32[65536,6]{1,0:T(8,128)} reshape(f32[65536,3,2]{2,1,0:T(4,128)} %bitcast.33) | data formatting | bytes 3145728
  793.1 5.0 reshape.308
  798.1 3.4 copy.45
  801.5 356.7 %reduce-scatter.9.cloned.1.call-done = f32[2048,6]{1,0:T(8,128)} async-done(((f32[65536,6]{1,0:T(8,128)}), f32[2048,6]{1,0:T(8,128)}) %reduce-scatter.9.cloned.1.call-update) | async-done | bytes 49168
  1158.1 5.0 reshape.310
  1163.2 3.4 copy.47
  (457 shorter events, 104.4 us)
Async XLA Ops:
  6.5 157.4 %all-gather.2.cloned.1.call-start = ((), (), s32[]{:S(2)}) async-start(), calls=%async_computation.2 | async-start | bytes 1622016 | tf_op jit(solution)/shard_map/all_gather | solution.py:56
  7.3 785.8 %reduce-scatter.7.cloned.1.call-start = ((), (), s32[]{:S(2)}) async-start(), calls=%async_computation.3 | async-start | bytes 5242880
  589.3 568.8 %reduce-scatter.9.cloned.1.call-start = ((), (), s32[]{:S(2)}) async-start(), calls=%async_computation.4 | async-start | bytes 34603008
Sparse Core Ops, SparseCore 0:
  9.0 154.8 all-gather.1
  589.4 51.6 reduce-scatter.6
  793.2 364.9 reduce-scatter.8
where the time goes:
time: 1180 us; the launch traced here: 1170 us
  waiting for transfers between devices  505 us (43%)
  local copies, waits for them, and re-layouts  293 us (25%)
  matrix products  210 us (18%)
  other arithmetic  142 us (12%)
  between operations  13.1 us (1%)
    unnamed x5, waiting for transfers between devices  357 us
    unnamed x8, local copies, waits for them, and re-layouts  248 us
    all_gather x1, waiting for transfers between devices, body(): col_pos = lax.all_gather(coords, 'rows', axis=2, tiled=True)  148 us
    dot_general x16, matrix products, tile_terms(): jnp.einsum('tij,tcj->tci', slopes, col_pos, precision=lax.Precision.HIGHEST)  114 us
    dot_general x16, matrix products, tile_terms(): jnp.einsum('tij,tci->tcj', slopes, row_pos, precision=lax.Precision.HIGHEST)  95.7 us
    reduce_sum x16, other arithmetic, tile_terms(): jnp.sum(slopes, axis=1)[:, None, :]  75.8 us
    gather x32, local copies, waits for them, and re-layouts, tile_step(): col_tile = col_blocks[:, :, local_cols]  32 us
    mul x16, other arithmetic, tile_terms(): observed = tile_counts.astype(jnp.float32) * factor  25.3 us
  transfers between devices with their start and end apart: 3, of which 2 were waited for; matrix products, arithmetic and copies ran while one was open for 18% of the time, Pallas kernels for 0%

commit v1 on v0

v1 whole, which is shorter than its diff:
```python
import functools

import jax
import jax.numpy as jnp
from jax import lax
from jax.experimental import pallas as pl
from jax.experimental.pallas import tpu as pltpu
from jax.sharding import Mesh
from jax.sharding import PartitionSpec as P

BETA_SAME = 8.0
BETA_OTHER = 2.0
REPULSE = 24.0
ALPHA = (4.0 / 3.0 * REPULSE) ** -0.5
B_SAME = BETA_SAME * ALPHA**1.5
B_OTHER = BETA_OTHER * ALPHA**1.5

ROWS = ("yl", "z", "x")
COLS = ("yh", "c")
LANES = 128
CHUNK = 128


def split3(x):
    hi = x.astype(jnp.bfloat16).astype(jnp.float32)
    rest = x - hi
    mid = rest.astype(jnp.bfloat16).astype(jnp.float32)
    return hi, mid, rest - mid


def unpack_tile(ref, tile, trial, quarters):
    parts = [ref[tile, pl.ds(trial * 3 * quarters + 3 * q, 3), :] for q in range(quarters)]
    pos = jnp.concatenate(parts, axis=1)
    return jnp.concatenate([pos, jnp.zeros((5, pos.shape[1]), jnp.float32)], axis=0)


def row_ids(width):
    return lax.broadcasted_iota(jnp.int32, (8, width), 0)


def put(base, values, first, width):
    ids = row_ids(width)
    for n, value in enumerate(values):
        base = jnp.where(ids == first + n, value, base)
    return base


def moment_rows(hi, mid, low):
    width = hi.shape[1]
    top = put(hi, [1.0], 3, width) + pltpu.roll(mid, 4, 0)
    return jnp.concatenate([top, low], axis=0).astype(jnp.bfloat16)


def distance_rows(pos, is_row):
    width = pos.shape[1]
    norm = ALPHA * jnp.sum(pos * pos, axis=0, keepdims=True)
    if is_row:
        hi, mid, low = split3(pos)
        first = put(hi, split3(norm), 3, width)
        second = put(mid, [1.0, 1.0, 1.0], 3, width)
        groups = [first, second, low, hi, mid, hi]
    else:
        hi, mid, low = split3((-2.0 * ALPHA) * pos)
        first = put(hi, [1.0, 1.0, 1.0], 3, width)
        second = put(hi, split3(norm + ALPHA), 3, width)
        groups = [first, second, hi, mid, mid, low]
    return jnp.concatenate(groups, axis=0)


def finish(total, pos):
    total = total[0:8] + total[8:16]
    total = total + pltpu.roll(total, 4, 0)
    return pos * total[3:4] - total


def add_tile(ref, tile, trial, grad, scale, quarters):
    for q in range(quarters):
        rows = pl.ds(trial * 3 * quarters + 3 * q, 3)
        ref[tile, rows, :] += scale * grad[0:3, q * LANES : (q + 1) * LANES]


def chrom_row(starts, first_bin, width):
    bins = first_bin + lax.broadcasted_iota(jnp.int32, (8, width), 1)
    total = jnp.zeros((8, width), jnp.int32)
    for n in range(starts.shape[0]):
        total += (bins >= starts[n]).astype(jnp.int32)
    return total


def kernel(
    group, columns, exponents, starts, row_ref, col_ref, counts_hbm,
    row_out, col_out, counts, sems, row_dist, row_moment, row_total,
):
    row_tiles, slots, tile_size = counts_hbm.shape[0], counts_hbm.shape[1], counts_hbm.shape[2]
    quarters = tile_size // LANES
    piece = row_tiles // group[2]
    scale = 3.0 * ALPHA / tile_size

    def copy(n):
        return pltpu.make_async_copy(counts_hbm.at[n // slots, n % slots], counts.at[n], sems.at[n])

    def start(n, carry):
        copy(n).start()
        return carry

    lax.fori_loop(0, row_tiles * slots, start, 0)
    row_out[...] = jnp.zeros_like(row_out)
    col_out[...] = jnp.zeros_like(col_out)

    def row_step(i, carry):
        row_pos = [unpack_tile(row_ref, i, t, quarters) for t in range(2)]
        for t in range(2):
            row_dist[t] = distance_rows(row_pos[t], True).T.astype(jnp.bfloat16)
            row_moment[t] = moment_rows(*split3(row_pos[t]))
            row_total[t] = jnp.zeros((16, tile_size), jnp.float32)
        row_tile = group[0] * row_tiles + i
        row_chrom = chrom_row(starts, row_tile * tile_size, tile_size)
        row_chrom = row_chrom.astype(jnp.float32).T[:, 0:1]

        for k in range(slots):
            n = i * slots + k
            copy(n).wait()
            column = columns[i, k]

            @pl.when(column >= 0)
            def _():
                local = column // (piece * group[2]) * piece + column % piece
                col_pos = [unpack_tile(col_ref, local, t, quarters) for t in range(2)]
                col_dist = [distance_rows(col_pos[t], False).astype(jnp.bfloat16) for t in range(2)]
                col_moment = [moment_rows(*split3(col_pos[t])) for t in range(2)]
                col_chrom = chrom_row(starts, column * tile_size, tile_size)[0:1].astype(jnp.float32)
                factor = jnp.exp2(jnp.full((1, LANES), -exponents[i, k], jnp.int32).astype(jnp.float32))[0:1, 0:1]
                col_total = [jnp.zeros((16, tile_size), jnp.float32) for t in range(2)]
                for c in range(tile_size // CHUNK):
                    rows = slice(c * CHUNK, (c + 1) * CHUNK)
                    observed = counts[n, rows, :].astype(jnp.float32) * factor
                    beta = jnp.where(row_chrom[rows] == col_chrom, B_SAME, B_OTHER)
                    for t in range(2):
                        s = jnp.dot(row_dist[t, rows, :], col_dist[t], preferred_element_type=jnp.float32)
                        r = lax.rsqrt(s)
                        r2 = r * r
                        w = r2 * (observed - r2 * (r * (beta + r)))
                        w = w.astype(jnp.bfloat16)
                        row_total[t, :, rows] += lax.dot_general(
                            col_moment[t], w, (((1,), (1,)), ((), ())), preferred_element_type=jnp.float32
                        )
                        col_total[t] += jnp.dot(row_moment[t, :, rows], w, preferred_element_type=jnp.float32)
                for t in range(2):
                    add_tile(col_out, local, t, finish(col_total[t], col_pos[t]), scale, quarters)

        for t in range(2):
            add_tile(row_out, i, t, finish(row_total[t], row_pos[t]), scale, quarters)
        return carry

    lax.fori_loop(0, row_tiles, row_step, 0)


def tile_gradients(group, columns, exponents, starts, row_pos, col_pos, counts):
    row_tiles, slots, tile_size = counts.shape[0], counts.shape[1], counts.shape[2]
    smem = pl.BlockSpec(memory_space=pltpu.SMEM)
    vmem = pl.BlockSpec(memory_space=pltpu.VMEM)
    return pl.pallas_call(
        kernel,
        out_shape=[
            jax.ShapeDtypeStruct(row_pos.shape, jnp.float32),
            jax.ShapeDtypeStruct(col_pos.shape, jnp.float32),
        ],
        in_specs=[smem] * 4 + [vmem] * 2 + [pl.BlockSpec(memory_space=pl.ANY)],
        out_specs=[vmem, vmem],
        scratch_shapes=[
            pltpu.VMEM((row_tiles * slots, tile_size, tile_size), jnp.bfloat16),
            pltpu.SemaphoreType.DMA((row_tiles * slots,)),
            pltpu.VMEM((2, tile_size, 48), jnp.bfloat16),
            pltpu.VMEM((2, 16, tile_size), jnp.bfloat16),
            pltpu.VMEM((2, 16, tile_size), jnp.float32),
        ],
        compiler_params=pltpu.CompilerParams(vmem_limit_bytes=48 * 1024 * 1024),
        name="tile_gradients",
    )(group, columns, exponents, starts, row_pos, col_pos, counts)


def body(coords, counts, tile_cols, exponents, chrom_starts):
    row_tiles, tile_size = counts.shape[0], counts.shape[2]
    width = coords.shape[2]
    tiles, quarters = width // tile_size, tile_size // LANES
    n_rows, n_cols = lax.axis_size(ROWS), lax.axis_size(COLS)
    local = coords.reshape(2, 3, tiles, quarters, LANES).transpose(2, 0, 3, 1, 4)
    local = local.reshape(tiles * 6 * quarters, LANES)
    row_pos = lax.all_gather(local, COLS, axis=0, tiled=True)
    col_pos = jnp.broadcast_to(local[None], (n_rows,) + local.shape)
    col_pos = lax.all_to_all(col_pos, ROWS, 0, 0, tiled=True)
    group = jnp.stack([lax.axis_index(ROWS), lax.axis_index(COLS), jnp.int32(n_cols)])
    row_part, col_part = tile_gradients(
        group, tile_cols, exponents, chrom_starts,
        row_pos.reshape(row_tiles, 6 * quarters, LANES),
        col_pos.reshape(n_rows * tiles, 6 * quarters, LANES),
        counts,
    )
    col_part = lax.all_to_all(col_part.reshape((n_rows,) + local.shape), ROWS, 0, 0, tiled=True)
    row_part = lax.all_to_all(row_part.reshape((n_cols,) + local.shape), COLS, 0, 0, tiled=True)
    grad = jnp.sum(col_part, axis=0) + jnp.sum(row_part, axis=0)
    grad = grad.reshape(tiles, 2, quarters, 3, LANES).transpose(1, 3, 0, 2, 4)
    return grad.reshape(2, 3, width)


def solution(mesh):
    fine = Mesh(mesh.devices.reshape(2, 4, 4, 2, 2), ROWS + COLS)
    placed = (
        P(None, None, ROWS + COLS),
        P(ROWS, COLS, None, None),
        P(ROWS, COLS),
        P(ROWS, COLS),
        P(),
    )
    return jax.shard_map(
        body, mesh=fine, in_specs=placed, out_specs=P(None, None, ROWS + COLS), check_vma=False
    )
```

time: 1180 us -> 138 us (0.12)
  waiting for transfers between devices: 505 us -> 29 us
  local copies, waits for them, and re-layouts: 293 us -> 3.13 us
  matrix products: 210 us -> 0 us
  other arithmetic: 142 us -> 0.18 us
  Pallas kernels: 0 us -> 55.6 us
  blocking collectives: 7.37 us -> 32.4 us
  starting transfers between devices: 0.26 us -> 17 us
  between operations: 13.1 us -> 0.1 us
    unnamed x5 -> x0, waiting for transfers between devices: 357 us -> none
    unnamed x8, local copies, waits for them, and re-layouts: 248 us -> 0.18 us
    dot_general x32 -> x0, matrix products: 210 us -> none  [the longest x16 114 us: tile_terms(): jnp.einsum('tij,tcj->tci', slopes, col_pos, precision=lax.Precision.HIGHEST)]
    all_gather x1 -> x0, waiting for transfers between devices: 148 us -> none  [body(): col_pos = lax.all_gather(coords, 'rows', axis=2, tiled=True)]
    reduce_sum x32 -> x2, other arithmetic: 88 us -> 0.1 us  [body(): grad = jnp.sum(col_part, axis=0) + jnp.sum(row_part, axis=0)]
    pallas_call x0 -> x1, Pallas kernels: none -> 55.6 us  [tile_gradients(): pl.pallas_call(kernel, out_shape=[jax.ShapeDtypeStruct(row_pos.shape, jnp...]
    gather x64 -> x0, local copies, waits for them, and re-layouts: 41.5 us -> none  [the longest x32 32 us: tile_step(): col_tile = col_blocks[:, :, local_cols]]
    all_to_all x0 -> x2, waiting for transfers between devices: none -> 29 us  [the longest x1 22.5 us: body(): lax.all_to_all(col_part.reshape((n_rows,) + local.shape), ROWS, 0, 0, til...]
  transfers between devices with their start and end apart: 3 -> 2, of which waited for: 2 -> 2; matrix products, arithmetic and copies ran while one was open for 18% -> 0% of each run, Pallas kernels for 0% -> 0%
where the time goes in v1:
time: 138 us; the launch traced here: 137 us
  Pallas kernels  55.6 us (40%)
  blocking collectives  32.4 us (23%)
  waiting for transfers between devices  29 us (21%)
  starting transfers between devices  17 us (12%)
  local copies, waits for them, and re-layouts  3.13 us (2%)
    pallas_call x1, Pallas kernels, tile_gradients(): pl.pallas_call(kernel, out_shape=[jax.ShapeDtypeStruct(row_pos.shape, jnp...  55.6 us
    all_to_all x1, waiting for transfers between devices, body(): lax.all_to_all(col_part.reshape((n_rows,) + local.shape), ROWS, 0, 0, til...  22.5 us
    all_to_all x1, blocking collectives, body(): lax.all_to_all(row_part.reshape((n_cols,) + local.shape), COLS, 0, 0, til...  16.6 us
    all_gather x1, blocking collectives, body(): row_pos = lax.all_gather(local, COLS, axis=0, tiled=True)  15.8 us
    all_to_all x1, starting transfers between devices, body(): col_pos = lax.all_to_all(col_pos, ROWS, 0, 0, tiled=True)  9.39 us
    all_to_all x1, starting transfers between devices, body(): lax.all_to_all(col_part.reshape((n_rows,) + local.shape), ROWS, 0, 0, til...  7.61 us
    all_to_all x1, waiting for transfers between devices, body(): col_pos = lax.all_to_all(col_pos, ROWS, 0, 0, tiled=True)  6.48 us
  transfers between devices with their start and end apart: 2, of which 2 were waited for; matrix products, arithmetic and copies ran while one was open for 0% of the time, Pallas kernels for 0%

profile of v1, /device:TPU:0, one launch (start us, length us, event | category | flops | bytes accessed | tf_op | source)
XLA Modules:
  0.0 137.4 jit_solution(4018048905602857905)
XLA Ops:
  0.0 0.8 reshape.26
  0.9 1.4 broadcast_in_dim.2
  2.3 0.0 copy-start.1
  2.3 0.0 copy-start.2
  2.3 0.0 copy-start
  2.3 9.4 %all-to-all-start = ((f32[32,96,128]{2,1,0:T(8,128)}), f32[32,96,128]{2,1,0:T(8,128)S(1)}, u32[]{:S(2)}, u32[]{:S(2)}) async-start(f32[32,96,128]{2,1,0:T(8,128)} %broadcast_in_dim.2), calls=%async_computation | async-start | bytes 3145728 | tf_op jit(solution)/shard_map/all_to_all | solution.py:191
  11.7 0.0 copy-done.1
  11.7 0.1 copy.13.columns
  11.8 0.0 copy-done.2
  11.8 0.1 copy.14.exponents
  11.9 15.8 %all_gather.3 = f32[384,128]{1,0:T(8,128)S(1)} all-gather(f32[96,128]{1,0:T(8,128)S(1)} %reshape.27), channel_id=1, replica_groups=mesh['yl'=2,'z'=4,'x'=4,'yh'=2,'c'=2] {'yh','c'}, dimensions={0}, use_global_device_ids=true | all-gather | bytes 245760 | tf_op jit(solution)/shard_map/all_gather | solution.py:189
  27.6 0.1 pad_add_fusion.group
  27.7 6.5 %all-to-all-done = f32[32,96,128]{2,1,0:T(8,128)S(1)} async-done(((f32[32,96,128]{2,1,0:T(8,128)}), f32[32,96,128]{2,1,0:T(8,128)S(1)}, u32[]{:S(2)}, u32[]{:S(2)}) %all-to-all-start) | async-done | bytes 1572896 | tf_op jit(solution)/shard_map/all_to_all | solution.py:191
  34.2 0.0 copy-done
  34.2 55.6 %tile_gradients.1 = (f32[16,24,128]{2,1,0:T(8,128)S(1)}, f32[128,24,128]{2,1,0:T(8,128)}) custom-call(s32[3]{0:T(128)S(1)} %pad_add_fusion.group, s32[16,2]{1,0:T(8,128)S(1)} %copy.13.columns, s32[16,2]{1,0:T(8,128)S(1)} %copy.14.exponents, s32[24]{0:T(128)S(1)} %copy-done, f32[16,24,128]{2,1,0:T(8,128)S(1)} %bitcast.15, f32[128,24,128]{2,1,0:T(8,128)S(1)} %bitcast.14, ...), custom_call_target="tpu_custom_call" | custom-call | tf_op jit(solution)/shard_map/tile_gradients/pallas_call | solution.py:162
  89.8 16.6 %all_to_all.15 = f32[4,96,128]{2,1,0:T(8,128)S(1)} all-to-all(f32[4,96,128]{2,1,0:T(8,128)S(1)} %bitcast.16), channel_id=1, replica_groups=mesh['yl'=2,'z'=4,'x'=4,'yh'=2,'c'=2] {'yh','c'}, dimensions={0} | all-to-all | bytes 393216 | tf_op jit(solution)/shard_map/all_to_all | solution.py:200
  106.5 7.6 %all-to-all-start.1 = ((f32[32,96,128]{2,1,0:T(8,128)}), f32[32,96,128]{2,1,0:T(8,128)S(1)}, u32[]{:S(2)}, u32[]{:S(2)}) async-start(f32[32,96,128]{2,1,0:T(8,128)} %bitcast.5), calls=%async_computation.1 | async-start | bytes 3145728 | tf_op jit(solution)/shard_map/all_to_all | solution.py:199
  114.1 22.5 %all-to-all-done.1 = f32[32,96,128]{2,1,0:T(8,128)S(1)} async-done(((f32[32,96,128]{2,1,0:T(8,128)}), f32[32,96,128]{2,1,0:T(8,128)S(1)}, u32[]{:S(2)}, u32[]{:S(2)}) %all-to-all-start.1) | async-done | bytes 1572896 | tf_op jit(solution)/shard_map/all_to_all | solution.py:199
  136.6 0.1 reduce_sum.18
  136.8 0.7 reshape.32
  (6 shorter events, 0.1 us)
Async XLA Ops:
  2.3 9.4 %copy-start.1 = (s32[16,2]{0,1:T(2,128)S(1)}, s32[16,2]{0,1:T(2,128)}, u32[]{:S(2)}) copy-start(s32[16,2]{0,1:T(2,128)} %param.7) | copy-start | bytes 388
  2.3 9.5 %copy-start.2 = (s32[16,2]{0,1:T(2,128)S(1)}, s32[16,2]{0,1:T(2,128)}, u32[]{:S(2)}) copy-start(s32[16,2]{0,1:T(2,128)} %param.8) | copy-start | bytes 388
  2.3 31.9 %copy-start = (s32[24]{0:T(128)S(1)}, s32[24]{0:T(128)}, u32[]{:S(2)}) copy-start(s32[24]{0:T(128)} %starts.1) | copy-start | bytes 292
  2.3 31.9 %all-to-all-start = ((f32[32,96,128]{2,1,0:T(8,128)}), f32[32,96,128]{2,1,0:T(8,128)S(1)}, u32[]{:S(2)}, u32[]{:S(2)}) async-start(f32[32,96,128]{2,1,0:T(8,128)} %broadcast_in_dim.2), calls=%async_computation | async-start | bytes 3145728 | tf_op jit(solution)/shard_map/all_to_all | solution.py:191
  106.5 30.2 %all-to-all-start.1 = ((f32[32,96,128]{2,1,0:T(8,128)}), f32[32,96,128]{2,1,0:T(8,128)S(1)}, u32[]{:S(2)}, u32[]{:S(2)}) async-start(f32[32,96,128]{2,1,0:T(8,128)} %bitcast.5), calls=%async_computation.1 | async-start | bytes 3145728 | tf_op jit(solution)/shard_map/all_to_all | solution.py:199

commit v2 on v1

v2 whole, which is shorter than its diff:
```python
import functools

import jax
import jax.numpy as jnp
from jax import lax
from jax.experimental import pallas as pl
from jax.experimental.pallas import tpu as pltpu
from jax.sharding import Mesh
from jax.sharding import PartitionSpec as P

BETA_SAME = 8.0
BETA_OTHER = 2.0
REPULSE = 24.0
EXPONENTS = (4, 5, 6, 7)
FACTORS = tuple(2.0**-e for e in EXPONENTS)
ALPHAS = tuple((f / (4.0 / 3.0 * REPULSE)) ** 0.5 for f in FACTORS)
HALF_ROOT = 0.5**0.5
ODD = tuple(e % 2 == 0 for e in EXPONENTS)
POWERS = tuple(2.0 ** -((e + 5) // 2) for e in EXPONENTS)
SLOPES = tuple(a**1.5 / f for a, f in zip(ALPHAS, FACTORS))
SCALES = tuple(3.0 * a * f for a, f in zip(ALPHAS, FACTORS))

ROWS = ("yl", "z", "x")
COLS = ("yh", "c")
LANES = 128
STEP = 32
GROUPS = 8
MOMENTS = 32


def pick(exponent, table):
    value = jnp.float32(table[-1])
    for e, entry in zip(EXPONENTS[-2::-1], table[-2::-1]):
        value = jnp.where(exponent <= e, jnp.float32(entry), value)
    return value


def split3(x):
    hi = x.astype(jnp.bfloat16).astype(jnp.float32)
    rest = x - hi
    mid = rest.astype(jnp.bfloat16).astype(jnp.float32)
    return hi, mid, rest - mid


def spread(tile):
    parts = [tile[6 * q : 6 * q + 6] for q in range(tile.shape[0] // 6)]
    wide = jnp.concatenate(parts, axis=1)
    return jnp.concatenate([wide, jnp.zeros((2, wide.shape[1]), jnp.float32)], axis=0)


def fold(wide):
    parts = [wide[0:6, q * LANES : (q + 1) * LANES] for q in range(wide.shape[1] // LANES)]
    return jnp.concatenate(parts, axis=0)


def row_ids(width):
    return lax.broadcasted_iota(jnp.int32, (8, width), 0)


def norms(pos):
    square = pos * pos
    return square + pltpu.roll(square, 7, 0) + pltpu.roll(square, 6, 0)


def moment_rows(hi, mid, low):
    ids = row_ids(hi.shape[1])
    top = jnp.where(ids == 6, 1.0, hi)
    return jnp.concatenate([top, mid, low, jnp.zeros_like(low)], axis=0).astype(jnp.bfloat16)


def norm_rows(norm):
    ids = row_ids(norm.shape[1])
    hi, mid, low = split3(norm)
    first = (ids == 0) | (ids == 3)
    second = (ids == 1) | (ids == 4)
    rows = jnp.where(first, hi, jnp.where(second, pltpu.roll(mid, 1, 0), pltpu.roll(low, 2, 0)))
    return rows, ids


def row_operand(pos):
    hi, mid, low = split3(pos)
    norm = norms(pos)
    rows, ids = norm_rows(norm)
    rows = jnp.where(ids >= 6, 1.0, rows)
    scaled, _ = norm_rows(norm * HALF_ROOT)
    scaled = jnp.where(ids == 6, 1.0, jnp.where(ids == 7, 0.0, scaled))
    operand = jnp.concatenate([hi, hi, mid, hi, mid, low, rows, scaled], axis=0)
    return operand, moment_rows(hi, mid, low)


def column_operand(pos, exponent):
    alpha = pick(exponent, ALPHAS)
    even = pick(exponent, [0.0 if odd else p for odd, p in zip(ODD, POWERS)])
    odd = pick(exponent, [p if odd else 0.0 for odd, p in zip(ODD, POWERS)])
    hi, mid, low = split3(pos * (-2.0 * alpha))
    norm = split3(alpha * (norms(pos) + 1.0))
    ids = row_ids(pos.shape[1])
    operands = []
    for t in range(2):
        mine = (ids < 3) if t == 0 else ((ids >= 3) & (ids < 6))
        h, m, l = [jnp.where(mine, x, 0.0) for x in (hi, mid, low)]
        up = [pltpu.roll(norm[n], (6 + n % 2 - 3 * t) % 8, 0) for n in range(3)]
        first = jnp.where(ids == 6, up[0], jnp.where(ids == 7, up[1], jnp.where(mine, even, 0.0)))
        second = jnp.where(ids == 6, up[2], jnp.where(mine, odd, 0.0))
        operands.append(jnp.concatenate([h, m, h, l, m, h, first, second], axis=0).astype(jnp.bfloat16))
    return operands, moment_rows(hi, mid, low)


def gather_moments(parts):
    sums = [p[0:8] + p[8:16] + p[16:24] for p in parts]
    ids = row_ids(sums[0].shape[1])
    return jnp.where(ids < 3, sums[0], sums[1]), jnp.where(ids < 3, sums[0][6:7], sums[1][6:7])


def chrom_row(starts, first_bin, width):
    bins = first_bin + lax.broadcasted_iota(jnp.int32, (8, width), 1)
    total = jnp.zeros((8, width), jnp.int32)
    for n in range(starts.shape[0]):
        total += (bins >= starts[n]).astype(jnp.int32)
    return total.astype(jnp.float32)


def kernel(window, group, columns, exponents, starts, *refs):
    if window:
        row_ref, counts_hbm, row_out = refs[:3]
        col_ref, col_out = row_ref, row_out
        scratch = refs[3:]
    else:
        row_ref, col_ref, counts_hbm, row_out, col_out = refs[:5]
        scratch = refs[5:]
    counts, sems, live, low_bin, high_bin, row_dist, row_mom, col_dist, col_mom, slopes, dist, half_row, half_col = scratch
    row_tiles, slots, tile_size = counts_hbm.shape[0], counts_hbm.shape[1], counts_hbm.shape[2]
    me, n_cols = group[1], group[2]
    piece = row_tiles // n_cols
    half = tile_size // 2
    row_first = group[0] * row_tiles
    contract_last = (((1,), (1,)), ((), ()))

    def copy(n):
        return pltpu.make_async_copy(counts_hbm.at[n // slots, n % slots], counts.at[n], sems.at[n])

    def start(n, total):
        i = n // slots
        column = columns[i, n % slots]
        is_own = column == row_first + i
        is_live = is_own if window else ((column >= 0) & jnp.logical_not(is_own))
        live[total] = n

        @pl.when(is_live)
        def _():
            copy(n).start()

        return total + is_live.astype(jnp.int32)

    live[0] = 0
    total = lax.fori_loop(0, row_tiles * slots, start, jnp.int32(0))
    row_out[...] = jnp.zeros_like(row_out)
    if not window:
        col_out[...] = jnp.zeros_like(col_out)
    slopes[1] = jnp.zeros(slopes.shape[1:], slopes.dtype)
    half_row[...] = jnp.zeros_like(half_row)
    half_col[...] = jnp.zeros_like(half_col)

    def prepare_row(i, carry):
        operand, moments = row_operand(spread(row_ref[i]))
        row_dist[i] = operand.T.astype(jnp.bfloat16)
        row_mom[i] = moments
        first = (row_first + (i // piece + me) % n_cols * piece + i % piece) * tile_size
        low, high = jnp.int32(0), jnp.int32(2**30)
        for n in range(starts.shape[0]):
            low = jnp.where(starts[n] <= first, starts[n], low)
        for n in range(starts.shape[0] - 1, -1, -1):
            high = jnp.where(starts[n] > first, starts[n], high)
        low_bin[i] = low
        high_bin[i] = high
        return carry

    lax.fori_loop(0, row_ref.shape[0], prepare_row, 0)

    def place(n):
        n = live[jnp.clip(n, 0, jnp.maximum(total - 1, 0))]
        i, k = n // slots, n % slots
        column = jnp.maximum(columns[i, k], 0)
        local = column // (piece * n_cols) * piece + column % piece
        if window:
            local = jnp.where(columns[i, k] == row_first + i, column % piece, 0)
        row = (i // piece - me + n_cols) % n_cols * piece + i % piece
        return n, jnp.minimum(row, row_ref.shape[0] - 1), column, local, exponents[i, k]

    def prepare_column(n):
        _, _, _, local, exponent = place(n)
        operands, moments = column_operand(spread(col_ref[local]), exponent)
        for t in range(2):
            col_dist[t] = operands[t]
        col_mom[1] = moments

    def distances(n, part):
        i = place(n)[1]
        for t in range(2):
            dist[part, t] = jnp.dot(
                row_dist[i, part * half : (part + 1) * half, :], col_dist[t], preferred_element_type=jnp.float32
            )

    def multiply(n, part):
        i = place(n)[1]
        rows = slice(part * half, (part + 1) * half)
        for t in range(2):
            w = slopes[part, t]
            half_row[t, :, rows] = lax.dot_general(
                col_mom[0], w, contract_last, preferred_element_type=jnp.float32
            )
            value = jnp.dot(row_mom[i, :, rows], w, preferred_element_type=jnp.float32)
            if part == 0:
                half_col[t] = value
            else:
                half_col[t] += value

    def finish(n):
        _, i, _, local, exponent = place(n)
        scale = pick(exponent, SCALES) * (1.0 / tile_size)
        back = pick(exponent, [-0.5 / a for a in ALPHAS])
        moment, weight = gather_moments([half_row[0], half_row[1]])
        row_out[i] += fold(scale * (spread(row_ref[i]) * weight - back * moment))
        moment, weight = gather_moments([half_col[0], half_col[1]])
        col_out[local] += fold(scale * (spread(col_ref[local]) * weight - moment))

    def elementwise(n, part, uniform):
        n, i, column, _, exponent = place(n)
        slope = pick(exponent, SLOPES)
        first = column * tile_size
        if uniform:
            bins = first + lax.broadcasted_iota(jnp.int32, (8, tile_size), 1)
            same = (bins >= low_bin[i]) & (bins < high_bin[i])
            beta = jnp.where(same, BETA_SAME * slope, BETA_OTHER * slope)
            beta = jnp.concatenate([beta] * (STEP // 8), axis=0)
        else:
            row_chrom = chrom_row(starts, (row_first + n // slots) * tile_size + part * half, half).T[:, 0:1]
            col_chrom = chrom_row(starts, first, tile_size)[0:1]
        for c in range(half // STEP):
            rows = slice(c * STEP, (c + 1) * STEP)
            observed = counts[n, part * half + c * STEP : part * half + (c + 1) * STEP, :].astype(jnp.float32)
            if not uniform:
                beta = jnp.where(row_chrom[rows] == col_chrom, BETA_SAME * slope, BETA_OTHER * slope)
            for t in range(2):
                r = lax.rsqrt(dist[part, t, rows, :])
                r2 = r * r
                w = r2 * (observed - r2 * (r * (beta + r)))
                slopes[part, t, rows, :] = w.astype(jnp.bfloat16)

    def step(n, uniform):
        distances(n, 1)
        elementwise(n, 0, uniform)
        multiply(n - 1, 1)
        finish(n - 1)
        col_mom[0] = col_mom[1]
        prepare_column(n + 1)
        distances(n + 1, 0)
        elementwise(n, 1, uniform)
        multiply(n, 0)

    prepare_column(0)
    distances(0, 0)
    col_mom[0] = jnp.zeros_like(col_mom[1])

    def loop(n, carry):
        slot, i, _, _, _ = place(n)
        copy(slot).wait()
        uniform = high_bin[i] >= (row_first + slot // slots + 1) * tile_size

        @pl.when(uniform)
        def _():
            step(n, True)

        @pl.when(jnp.logical_not(uniform))
        def _():
            step(n, False)

        return carry

    lax.fori_loop(0, total, loop, 0)
    multiply(total - 1, 1)
    finish(total - 1)


def scratch_of(counts, rows):
    row_tiles, slots, tile_size = counts.shape[0], counts.shape[1], counts.shape[2]
    half = tile_size // 2
    return [
        pltpu.VMEM((row_tiles * slots, tile_size, tile_size), jnp.bfloat16),
        pltpu.SemaphoreType.DMA((row_tiles * slots,)),
        pltpu.SMEM((row_tiles * slots + 1,), jnp.int32),
        pltpu.SMEM((rows,), jnp.int32),
        pltpu.SMEM((rows,), jnp.int32),
        pltpu.VMEM((rows, tile_size, 8 * GROUPS), jnp.bfloat16),
        pltpu.VMEM((rows, MOMENTS, tile_size), jnp.bfloat16),
        pltpu.VMEM((2, 8 * GROUPS, tile_size), jnp.bfloat16),
        pltpu.VMEM((2, MOMENTS, tile_size), jnp.bfloat16),
        pltpu.VMEM((2, 2, half, tile_size), jnp.bfloat16),
        pltpu.VMEM((2, 2, half, tile_size), jnp.float32),
        pltpu.VMEM((2, MOMENTS, tile_size), jnp.float32),
        pltpu.VMEM((2, MOMENTS, tile_size), jnp.float32),
    ]


SMEM = pl.BlockSpec(memory_space=pltpu.SMEM)
VMEM = pl.BlockSpec(memory_space=pltpu.VMEM)
PARAMS = pltpu.CompilerParams(vmem_limit_bytes=44 * 1024 * 1024)


def own_gradients(group, columns, exponents, starts, own_pos, counts):
    return pl.pallas_call(
        functools.partial(kernel, True),
        out_shape=jax.ShapeDtypeStruct(own_pos.shape, jnp.float32),
        in_specs=[SMEM] * 4 + [VMEM, pl.BlockSpec(memory_space=pl.ANY)],
        out_specs=VMEM,
        scratch_shapes=scratch_of(counts, own_pos.shape[0]),
        compiler_params=PARAMS,
        name="own_gradients",
    )(group, columns, exponents, starts, own_pos, counts)


def tile_gradients(group, columns, exponents, starts, row_pos, col_pos, counts):
    return pl.pallas_call(
        functools.partial(kernel, False),
        out_shape=[
            jax.ShapeDtypeStruct(row_pos.shape, jnp.float32),
            jax.ShapeDtypeStruct(col_pos.shape, jnp.float32),
        ],
        in_specs=[SMEM] * 4 + [VMEM] * 2 + [pl.BlockSpec(memory_space=pl.ANY)],
        out_specs=[VMEM, VMEM],
        scratch_shapes=scratch_of(counts, row_pos.shape[0]),
        compiler_params=PARAMS,
        name="tile_gradients",
    )(group, columns, exponents, starts, row_pos, col_pos, counts)


def body(coords, counts, tile_cols, exponents, chrom_starts):
    row_tiles, tile_size = counts.shape[0], counts.shape[2]
    width = coords.shape[2]
    tiles, quarters = width // tile_size, tile_size // LANES
    n_rows, n_cols = lax.axis_size(ROWS), lax.axis_size(COLS)
    local = coords.reshape(2, 3, tiles, quarters, LANES).transpose(2, 3, 0, 1, 4)
    local = local.reshape(tiles, 6 * quarters, LANES)
    col_pos = jnp.broadcast_to(local[None], (n_rows,) + local.shape)
    col_pos = lax.all_to_all(col_pos, ROWS, 0, 0, tiled=True).reshape((n_rows * tiles,) + local.shape[1:])
    pieces = [
        lax.ppermute(local, COLS, [((g + shift) % n_cols, g) for g in range(n_cols)]) for shift in range(1, n_cols)
    ]
    row_pos = jnp.concatenate([local] + pieces, axis=0)
    group = jnp.stack([lax.axis_index(ROWS), lax.axis_index(COLS), jnp.int32(n_cols)])
    own_part = own_gradients(group, tile_cols, exponents, chrom_starts, local, counts)
    row_part, col_part = tile_gradients(group, tile_cols, exponents, chrom_starts, row_pos, col_pos, counts)
    col_part = lax.all_to_all(col_part.reshape((n_rows,) + local.shape), ROWS, 0, 0, tiled=True)
    row_sum = own_part + row_part[:tiles]
    for shift in range(1, n_cols):
        piece = row_part[shift * tiles : (shift + 1) * tiles]
        row_sum += lax.ppermute(piece, COLS, [(g, (g + shift) % n_cols) for g in range(n_cols)])
    grad = jnp.sum(col_part, axis=0) + row_sum
    grad = grad.reshape(tiles, quarters, 2, 3, LANES).transpose(2, 3, 0, 1, 4)
    return grad.reshape(2, 3, width)


def solution(mesh):
    fine = Mesh(mesh.devices.reshape(2, 4, 4, 2, 2), ROWS + COLS)
    placed = (
        P(None, None, ROWS + COLS),
        P(ROWS, COLS, None, None),
        P(ROWS, COLS),
        P(ROWS, COLS),
        P(),
    )
    return jax.shard_map(
        body, mesh=fine, in_specs=placed, out_specs=P(None, None, ROWS + COLS), check_vma=False
    )
```

time: 138 us -> 96.2 us (0.70)
  blocking collectives: 32.4 us -> 0 us
  Pallas kernels: 55.6 us -> 36.5 us
  starting transfers between devices: 17 us -> 31 us
  waiting for transfers between devices: 29 us -> 24.6 us
    pallas_call x1 -> x2, Pallas kernels: 55.6 us -> 36.5 us  [the longest x1 29.5 us: tile_gradients(): pl.pallas_call(functools.partial(kernel, False), out_shape=[jax.ShapeDtyp...]
    all_to_all x1 -> x0, blocking collectives: 16.6 us -> none  [body(): lax.all_to_all(row_part.reshape((n_cols,) + local.shape), COLS, 0, 0, til...]
    all_gather x1 -> x0, blocking collectives: 15.8 us -> none  [body(): row_pos = lax.all_gather(local, COLS, axis=0, tiled=True)]
    all_to_all x1, waiting for transfers between devices: 22.5 us -> 8.27 us  [body(): lax.all_to_all(col_part.reshape((n_rows,) + local.shape), ROWS, 0, 0, til...]
    ppermute x0 -> x6, waiting for transfers between devices: none -> 12.3 us  [the longest x3 12.3 us: body(): lax.ppermute(local, COLS, [((g + shift) % n_cols, g) for g in range(n_col...]
    ppermute x0 -> x6, starting transfers between devices: none -> 11.7 us  [the longest x3 5.93 us: body(): lax.ppermute(local, COLS, [((g + shift) % n_cols, g) for g in range(n_col...]
    all_to_all x1, waiting for transfers between devices: 6.48 us -> 3.97 us  [body(): lax.all_to_all(col_pos, ROWS, 0, 0, tiled=True)]
    all_to_all x1, starting transfers between devices: 7.61 us -> 9.92 us  [body(): lax.all_to_all(col_part.reshape((n_rows,) + local.shape), ROWS, 0, 0, til...]
  transfers between devices with their start and end apart: 2 -> 8, of which waited for: 2 -> 4; matrix products, arithmetic and copies ran while one was open for 0% -> 0% of each run, Pallas kernels for 0% -> 7%
where the time goes in v2:
time: 96.2 us; the launch traced here: 95.5 us
  Pallas kernels  36.5 us (38%)
  starting transfers between devices  31 us (32%)
  waiting for transfers between devices  24.6 us (26%)
  local copies, waits for them, and re-layouts  3.09 us (3%)
    pallas_call x1, Pallas kernels, tile_gradients(): pl.pallas_call(functools.partial(kernel, False), out_shape=[jax.ShapeDtyp...  29.5 us
    ppermute x3, waiting for transfers between devices, body(): lax.ppermute(local, COLS, [((g + shift) % n_cols, g) for g in range(n_col...  12.3 us
    all_to_all x1, starting transfers between devices, body(): lax.all_to_all(col_part.reshape((n_rows,) + local.shape), ROWS, 0, 0, til...  9.92 us
    all_to_all x1, starting transfers between devices, body(): lax.all_to_all(col_pos, ROWS, 0, 0, tiled=True)  9.39 us
    all_to_all x1, waiting for transfers between devices, body(): lax.all_to_all(col_part.reshape((n_rows,) + local.shape), ROWS, 0, 0, til...  8.27 us
    pallas_call x1, Pallas kernels, own_gradients(): pl.pallas_call(functools.partial(kernel, True), out_shape=jax.ShapeDtypeS...  7 us
    ppermute x3, starting transfers between devices, body(): lax.ppermute(local, COLS, [((g + shift) % n_cols, g) for g in range(n_col...  5.93 us
    ppermute x3, starting transfers between devices, body(): lax.ppermute(piece, COLS, [(g, (g + shift) % n_cols) for g in range(n_col...  5.75 us
  transfers between devices with their start and end apart: 8, of which 4 were waited for; matrix products, arithmetic and copies ran while one was open for 0% of the time, Pallas kernels for 7%

profile of v2, /device:TPU:0, one launch (start us, length us, event | category | flops | bytes accessed | tf_op | source)
XLA Modules:
  0.0 95.5 jit_solution(11918359692443286469)
XLA Ops:
  0.0 0.8 reshape.19
  0.9 1.4 %broadcast_in_dim.2 = f32[32,4,24,128]{3,2,1,0:T(8,128)} broadcast(f32[4,24,128]{2,1,0:T(8,128)S(1)} %copy.28.refs_0_), dimensions={1,2,3} | broadcast | bytes 1622016 | tf_op jit(solution)/shard_map/broadcast_in_dim | solution.py:344
  2.2 0.0 copy-start.1
  2.2 0.0 copy-start.2
  2.2 0.0 copy-start
  2.2 9.4 %all-to-all-start = ((f32[32,4,24,128]{3,2,1,0:T(8,128)}), f32[32,4,24,128]{3,2,1,0:T(8,128)S(1)}, u32[]{:S(2)}, u32[]{:S(2)}) async-start(f32[32,4,24,128]{3,2,1,0:T(8,128)} %broadcast_in_dim.2), calls=%async_computation | async-start | bytes 3145728 | tf_op jit(solution)/shard_map/all_to_all | solution.py:345
  11.6 0.1 collective-permute-start.2
  11.7 3.0 %collective-permute-start.1 = (f32[4,24,128]{2,1,0:T(8,128)S(1)}, f32[4,24,128]{2,1,0:T(8,128)S(1)}, u32[]{:S(2)}, u32[]{:S(2)}) collective-permute-start(f32[4,24,128]{2,1,0:T(8,128)S(1)} %copy.28.refs_0_), channel_id=1, source_target_pairs={{2,0},{3,1},{0,2},{1,3},{6,4},{7,5},{4,6},{5,7},{10,8},{11,9},{8,1... | collective-permute-start | bytes 147464 | tf_op jit(solution)/shard_map/ppermute | solution.py:347
  14.7 2.9 %collective-permute-start = (f32[4,24,128]{2,1,0:T(8,128)S(1)}, f32[4,24,128]{2,1,0:T(8,128)S(1)}, u32[]{:S(2)}, u32[]{:S(2)}) collective-permute-start(f32[4,24,128]{2,1,0:T(8,128)S(1)} %copy.28.refs_0_), channel_id=1, source_target_pairs={{1,0},{2,1},{3,2},{0,3},{5,4},{6,5},{7,6},{4,7},{9,8},{10,9},{11,1... | collective-permute-start | bytes 147464 | tf_op jit(solution)/shard_map/ppermute | solution.py:347
  17.6 0.1 pad_add_fusion.group
  17.7 0.0 copy-done.1
  17.7 0.1 copy.30.columns
  17.7 0.0 copy-done.2
  17.7 0.1 copy.31.exponents
  17.8 3.5 %collective-permute-done.2 = f32[4,24,128]{2,1,0:T(8,128)S(1)} collective-permute-done((f32[4,24,128]{2,1,0:T(8,128)S(1)}, f32[4,24,128]{2,1,0:T(8,128)S(1)}, u32[]{:S(2)}, u32[]{:S(2)}) %collective-permute-start.2) | collective-permute-done | bytes 49184 | tf_op jit(solution)/shard_map/ppermute | solution.py:347
  21.3 8.8 %collective-permute-done.1 = f32[4,24,128]{2,1,0:T(8,128)S(1)} collective-permute-done((f32[4,24,128]{2,1,0:T(8,128)S(1)}, f32[4,24,128]{2,1,0:T(8,128)S(1)}, u32[]{:S(2)}, u32[]{:S(2)}) %collective-permute-start.1) | collective-permute-done | bytes 49184 | tf_op jit(solution)/shard_map/ppermute | solution.py:347
  30.2 0.0 collective-permute-done
  30.2 4.0 %all-to-all-done = f32[32,4,24,128]{3,2,1,0:T(8,128)S(1)} async-done(((f32[32,4,24,128]{3,2,1,0:T(8,128)}), f32[32,4,24,128]{3,2,1,0:T(8,128)S(1)}, u32[]{:S(2)}, u32[]{:S(2)}) %all-to-all-start) | async-done | bytes 1572896 | tf_op jit(solution)/shard_map/all_to_all | solution.py:345
  34.1 0.0 copy-done
  34.1 29.5 %tile_gradients.1 = (f32[16,24,128]{2,1,0:T(8,128)S(1)}, f32[128,24,128]{2,1,0:T(8,128)}) custom-call(s32[3]{0:T(128)S(1)} %pad_add_fusion.group, s32[16,2]{1,0:T(8,128)S(1)} %copy.30.columns, s32[16,2]{1,0:T(8,128)S(1)} %copy.31.exponents, s32[24]{0:T(128)S(1)} %copy-done, f32[16,24,128]{2,1,0:T(8,128)S(1)} %pad_maximum_fusion.refs_0_, ...), custom_call_target="tpu_custom_call" | custom-call | tf_op jit(solution)/shard_map/tile_gradients/pallas_call | solution.py:323
  63.6 9.9 %all-to-all-start.1 = ((f32[32,4,24,128]{3,2,1,0:T(8,128)}), f32[32,4,24,128]{3,2,1,0:T(8,128)S(1)}, u32[]{:S(2)}, u32[]{:S(2)}) async-start(f32[32,4,24,128]{3,2,1,0:T(8,128)} %bitcast.5), calls=%async_computation.1 | async-start | bytes 3145728 | tf_op jit(solution)/shard_map/all_to_all | solution.py:353
  73.6 0.1 collective-permute-start.3
  73.7 3.2 %collective-permute-start.5 = (f32[4,24,128]{2,1,0:T(8,128)S(1)}, f32[4,24,128]{2,1,0:T(8,128)S(1)}, u32[]{:S(2)}, u32[]{:S(2)}) collective-permute-start(f32[4,24,128]{2,1,0:T(8,128)S(1)} %get-tuple-element.10), channel_id=1, source_target_pairs={{0,3},{1,0},{2,1},{3,2},{4,7},{5,4},{6,5},{7,6},{8,11},{9,8},{10,9... | collective-permute-start | bytes 147464 | tf_op jit(solution)/shard_map/ppermute | solution.py:357
  76.9 2.4 %collective-permute-start.4 = (f32[4,24,128]{2,1,0:T(8,128)S(1)}, f32[4,24,128]{2,1,0:T(8,128)S(1)}, u32[]{:S(2)}, u32[]{:S(2)}) collective-permute-start(f32[4,24,128]{2,1,0:T(8,128)S(1)} %get-tuple-element.11), channel_id=1, source_target_pairs={{0,2},{1,3},{2,0},{3,1},{4,6},{5,7},{6,4},{7,5},{8,10},{9,11},{10,... | collective-permute-start | bytes 147464 | tf_op jit(solution)/shard_map/ppermute | solution.py:357
  79.3 7.0 %own_gradients.1 = f32[4,24,128]{2,1,0:T(8,128)S(1)} custom-call(s32[3]{0:T(128)S(1)} %pad_add_fusion.group, s32[16,2]{1,0:T(8,128)S(1)} %copy.30.columns, s32[16,2]{1,0:T(8,128)S(1)} %copy.31.exponents, s32[24]{0:T(128)S(1)} %copy-done, f32[4,24,128]{2,1,0:T(8,128)S(1)} %copy.28.refs_0_, bf16[16,2,512,512]{3,2,1,0:T(8,128)(2,1)} %refs_1_.1), custom_call_target="tpu_custom_call" | custom-call | tf_op jit(solution)/shard_map/own_gradients/pallas_call | solution.py:311
  86.3 8.3 %all-to-all-done.1 = f32[32,4,24,128]{3,2,1,0:T(8,128)S(1)} async-done(((f32[32,4,24,128]{3,2,1,0:T(8,128)}), f32[32,4,24,128]{3,2,1,0:T(8,128)S(1)}, u32[]{:S(2)}, u32[]{:S(2)}) %all-to-all-start.1) | async-done | bytes 1572896 | tf_op jit(solution)/shard_map/all_to_all | solution.py:353
  94.6 0.1 reduce_sum.9
  94.7 0.0 collective-permute-done.3
  94.7 0.0 collective-permute-done.5
  94.7 0.0 collective-permute-done.4
  94.8 0.7 reshape.24
  (7 shorter events, 0.1 us)
Async XLA Ops:
  2.2 15.4 %copy-start.1 = (s32[16,2]{0,1:T(2,128)S(1)}, s32[16,2]{0,1:T(2,128)}, u32[]{:S(2)}) copy-start(s32[16,2]{0,1:T(2,128)} %param.7) | copy-start | bytes 388
  2.2 15.5 %copy-start.2 = (s32[16,2]{0,1:T(2,128)S(1)}, s32[16,2]{0,1:T(2,128)}, u32[]{:S(2)}) copy-start(s32[16,2]{0,1:T(2,128)} %param.8) | copy-start | bytes 388
  2.2 31.9 %copy-start = (s32[24]{0:T(128)S(1)}, s32[24]{0:T(128)}, u32[]{:S(2)}) copy-start(s32[24]{0:T(128)} %starts.3) | copy-start | bytes 292
  2.2 31.9 %all-to-all-start = ((f32[32,4,24,128]{3,2,1,0:T(8,128)}), f32[32,4,24,128]{3,2,1,0:T(8,128)S(1)}, u32[]{:S(2)}, u32[]{:S(2)}) async-start(f32[32,4,24,128]{3,2,1,0:T(8,128)} %broadcast_in_dim.2), calls=%async_computation | async-start | bytes 3145728 | tf_op jit(solution)/shard_map/all_to_all | solution.py:345
  11.6 9.7 %collective-permute-start.2 = (f32[4,24,128]{2,1,0:T(8,128)S(1)}, f32[4,24,128]{2,1,0:T(8,128)S(1)}, u32[]{:S(2)}, u32[]{:S(2)}) collective-permute-start(f32[4,24,128]{2,1,0:T(8,128)S(1)} %copy.28.refs_0_), channel_id=1, source_target_pairs={{3,0},{0,1},{1,2},{2,3},{7,4},{4,5},{5,6},{6,7},{11,8},{8,9},{9,10... | collective-permute-start | bytes 147464 | tf_op jit(solution)/shard_map/ppermute | solution.py:347
  11.7 18.4 %collective-permute-start.1 = (f32[4,24,128]{2,1,0:T(8,128)S(1)}, f32[4,24,128]{2,1,0:T(8,128)S(1)}, u32[]{:S(2)}, u32[]{:S(2)}) collective-permute-start(f32[4,24,128]{2,1,0:T(8,128)S(1)} %copy.28.refs_0_), channel_id=1, source_target_pairs={{2,0},{3,1},{0,2},{1,3},{6,4},{7,5},{4,6},{5,7},{10,8},{11,9},{8,1... | collective-permute-start | bytes 147464 | tf_op jit(solution)/shard_map/ppermute | solution.py:347
  14.7 15.4 %collective-permute-start = (f32[4,24,128]{2,1,0:T(8,128)S(1)}, f32[4,24,128]{2,1,0:T(8,128)S(1)}, u32[]{:S(2)}, u32[]{:S(2)}) collective-permute-start(f32[4,24,128]{2,1,0:T(8,128)S(1)} %copy.28.refs_0_), channel_id=1, source_target_pairs={{1,0},{2,1},{3,2},{0,3},{5,4},{6,5},{7,6},{4,7},{9,8},{10,9},{11,1... | collective-permute-start | bytes 147464 | tf_op jit(solution)/shard_map/ppermute | solution.py:347
  63.6 31.0 %all-to-all-start.1 = ((f32[32,4,24,128]{3,2,1,0:T(8,128)}), f32[32,4,24,128]{3,2,1,0:T(8,128)S(1)}, u32[]{:S(2)}, u32[]{:S(2)}) async-start(f32[32,4,24,128]{3,2,1,0:T(8,128)} %bitcast.5), calls=%async_computation.1 | async-start | bytes 3145728 | tf_op jit(solution)/shard_map/all_to_all | solution.py:353
  73.6 21.1 %collective-permute-start.3 = (f32[4,24,128]{2,1,0:T(8,128)S(1)}, f32[4,24,128]{2,1,0:T(8,128)S(1)}, u32[]{:S(2)}, u32[]{:S(2)}) collective-permute-start(f32[4,24,128]{2,1,0:T(8,128)S(1)} %get-tuple-element.9), channel_id=1, source_target_pairs={{0,1},{1,2},{2,3},{3,0},{4,5},{5,6},{6,7},{7,4},{8,9},{9,10},{10,1... | collective-permute-start | bytes 147464 | tf_op jit(solution)/shard_map/ppermute | solution.py:357
  73.7 21.1 %collective-permute-start.5 = (f32[4,24,128]{2,1,0:T(8,128)S(1)}, f32[4,24,128]{2,1,0:T(8,128)S(1)}, u32[]{:S(2)}, u32[]{:S(2)}) collective-permute-start(f32[4,24,128]{2,1,0:T(8,128)S(1)} %get-tuple-element.10), channel_id=1, source_target_pairs={{0,3},{1,0},{2,1},{3,2},{4,7},{5,4},{6,5},{7,6},{8,11},{9,8},{10,9... | collective-permute-start | bytes 147464 | tf_op jit(solution)/shard_map/ppermute | solution.py:357
  76.9 17.8 %collective-permute-start.4 = (f32[4,24,128]{2,1,0:T(8,128)S(1)}, f32[4,24,128]{2,1,0:T(8,128)S(1)}, u32[]{:S(2)}, u32[]{:S(2)}) collective-permute-start(f32[4,24,128]{2,1,0:T(8,128)S(1)} %get-tuple-element.11), channel_id=1, source_target_pairs={{0,2},{1,3},{2,0},{3,1},{4,6},{5,7},{6,4},{7,5},{8,10},{9,11},{10,... | collective-permute-start | bytes 147464 | tf_op jit(solution)/shard_map/ppermute | solution.py:357

commit v3 on v2

--- a/solution.py
+++ b/solution.py
@@ -24,8 +24,10 @@
 COLS = ("yh", "c")
 LANES = 128
 STEP = 32
-GROUPS = 8
-MOMENTS = 32
+GROUPS = 4
+MOMENTS = 16
+AHEAD = 6
+TOGETHER = 4
 
 
 def pick(exponent, table):
@@ -62,10 +64,22 @@
     return square + pltpu.roll(square, 7, 0) + pltpu.roll(square, 6, 0)
 
 
-def moment_rows(hi, mid, low):
+def own_rows(low, high, trial):
+    ids = row_ids(low.shape[1])
+    if trial == 0:
+        high = pltpu.roll(high, 3, 0)
+    else:
+        low = pltpu.roll(low, 5, 0)
+    return jnp.where(ids < 3, low, jnp.where(ids < 6, high, 0.0))
+
+
+def moment_rows(hi, mid, low, trial):
     ids = row_ids(hi.shape[1])
-    top = jnp.where(ids == 6, 1.0, hi)
-    return jnp.concatenate([top, mid, low, jnp.zeros_like(low)], axis=0).astype(jnp.bfloat16)
+    if trial == 1:
+        hi, low = pltpu.roll(hi, 5, 0), pltpu.roll(low, 5, 0)
+    mid = pltpu.roll(mid, 4 - 3 * trial, 0)
+    top = jnp.where(ids < 3, hi, jnp.where(ids == 3, 1.0, jnp.where(ids < 7, mid, 0.0)))
+    return jnp.concatenate([top, jnp.where(ids < 3, low, 0.0)], axis=0).astype(jnp.bfloat16)
 
 
 def norm_rows(norm):
@@ -81,11 +95,15 @@
     hi, mid, low = split3(pos)
     norm = norms(pos)
     rows, ids = norm_rows(norm)
-    rows = jnp.where(ids >= 6, 1.0, rows)
     scaled, _ = norm_rows(norm * HALF_ROOT)
-    scaled = jnp.where(ids == 6, 1.0, jnp.where(ids == 7, 0.0, scaled))
-    operand = jnp.concatenate([hi, hi, mid, hi, mid, low, rows, scaled], axis=0)
-    return operand, moment_rows(hi, mid, low)
+    operands, moments = [], []
+    for t in range(2):
+        first = jnp.where(ids >= 6, 1.0, own_rows(hi, hi, t))
+        second = jnp.where(ids == 6, 1.0, own_rows(mid, hi, t))
+        operand = jnp.concatenate([first, second, own_rows(mid, low, t), own_rows(rows, scaled, t)], axis=0)
+        operands.append(operand.astype(jnp.bfloat16))
+        moments.append(moment_rows(hi, mid, low, t))
+    return operands, moments
 
 
 def column_operand(pos, exponent):
@@ -95,21 +113,24 @@
     hi, mid, low = split3(pos * (-2.0 * alpha))
     norm = split3(alpha * (norms(pos) + 1.0))
     ids = row_ids(pos.shape[1])
-    operands = []
+    powers = jnp.where(ids < 3, even, jnp.where(ids < 6, odd, 0.0))
+    operands, moments = [], []
     for t in range(2):
-        mine = (ids < 3) if t == 0 else ((ids >= 3) & (ids < 6))
-        h, m, l = [jnp.where(mine, x, 0.0) for x in (hi, mid, low)]
         up = [pltpu.roll(norm[n], (6 + n % 2 - 3 * t) % 8, 0) for n in range(3)]
-        first = jnp.where(ids == 6, up[0], jnp.where(ids == 7, up[1], jnp.where(mine, even, 0.0)))
-        second = jnp.where(ids == 6, up[2], jnp.where(mine, odd, 0.0))
-        operands.append(jnp.concatenate([h, m, h, l, m, h, first, second], axis=0).astype(jnp.bfloat16))
-    return operands, moment_rows(hi, mid, low)
+        first = jnp.where(ids == 6, up[0], jnp.where(ids == 7, up[1], own_rows(hi, mid, t)))
+        second = jnp.where(ids == 6, up[2], own_rows(hi, low, t))
+        operand = jnp.concatenate([first, second, own_rows(mid, hi, t), powers], axis=0)
+        operands.append(operand.astype(jnp.bfloat16))
+        moments.append(moment_rows(hi, mid, low, t))
+    return operands, moments
 
 
 def gather_moments(parts):
-    sums = [p[0:8] + p[8:16] + p[16:24] for p in parts]
+    sums = [p[0:8] + p[8:16] for p in parts]
+    sums = [p + pltpu.roll(p, 4, 0) for p in sums]
     ids = row_ids(sums[0].shape[1])
-    return jnp.where(ids < 3, sums[0], sums[1]), jnp.where(ids < 3, sums[0][6:7], sums[1][6:7])
+    moment = jnp.where(ids < 3, sums[0], pltpu.roll(sums[1], 3, 0))
+    return moment, jnp.where(ids < 3, sums[0][3:4], sums[1][3:4])
 
 
 def chrom_row(starts, first_bin, width):
@@ -146,7 +167,7 @@
         is_live = is_own if window else ((column >= 0) & jnp.logical_not(is_own))
         live[total] = n
 
-        @pl.when(is_live)
+        @pl.when(is_live & (total < AHEAD))
         def _():
             copy(n).start()
 
@@ -162,9 +183,10 @@
     half_col[...] = jnp.zeros_like(half_col)
 
     def prepare_row(i, carry):
-        operand, moments = row_operand(spread(row_ref[i]))
-        row_dist[i] = operand.T.astype(jnp.bfloat16)
-        row_mom[i] = moments
+        operands, moments = row_operand(spread(row_ref[i]))
+        for t in range(2):
+            row_dist[i, t] = operands[t].T
+            row_mom[i, t] = moments[t]
         first = (row_first + (i // piece + me) % n_cols * piece + i % piece) * tile_size
         low, high = jnp.int32(0), jnp.int32(2**30)
         for n in range(starts.shape[0]):
@@ -175,7 +197,7 @@
         high_bin[i] = high
         return carry
 
-    lax.fori_loop(0, row_ref.shape[0], prepare_row, 0)
+    lax.fori_loop(0, row_ref.shape[0], prepare_row, 0, unroll=4)
 
     def place(n):
         n = live[jnp.clip(n, 0, jnp.maximum(total - 1, 0))]
@@ -192,13 +214,13 @@
         operands, moments = column_operand(spread(col_ref[local]), exponent)
         for t in range(2):
             col_dist[t] = operands[t]
-        col_mom[1] = moments
+            col_mom[1, t] = moments[t]
 
     def distances(n, part):
         i = place(n)[1]
         for t in range(2):
             dist[part, t] = jnp.dot(
-                row_dist[i, part * half : (part + 1) * half, :], col_dist[t], preferred_element_type=jnp.float32
+                row_dist[i, t, part * half : (part + 1) * half, :], col_dist[t], preferred_element_type=jnp.float32
             )
 
     def multiply(n, part):
@@ -207,9 +229,15 @@
         for t in range(2):
             w = slopes[part, t]
             half_row[t, :, rows] = lax.dot_general(
-                col_mom[0], w, contract_last, preferred_element_type=jnp.float32
+                col_mom[0, t], w, contract_last, preferred_element_type=jnp.float32
             )
-            value = jnp.dot(row_mom[i, :, rows], w, preferred_element_type=jnp.float32)
+            value = jnp.concatenate(
+                [
+                    jnp.dot(row_mom[i, t, :, rows], slopes[part, t, :, lanes], preferred_element_type=jnp.float32)
+                    for lanes in (slice(0, half), slice(half, tile_size))
+                ],
+                axis=1,
+            )
             if part == 0:
                 half_col[t] = value
             else:
@@ -262,22 +290,41 @@
     distances(0, 0)
     col_mom[0] = jnp.zeros_like(col_mom[1])
 
+    def arrive(n):
+        slot, i, _, _, _ = place(n)
+
+        @pl.when(n < total)
+        def _():
+            copy(slot).wait()
+
+        @pl.when(n + AHEAD < total)
+        def _():
+            copy(live[n + AHEAD]).start()
+
+        return high_bin[i] >= (row_first + slot // slots + 1) * tile_size
+
+    def general(n, carry):
+        step(n, False)
+        return carry
+
     def loop(n, carry):
-        slot, i, _, _, _ = place(n)
-        copy(slot).wait()
-        uniform = high_bin[i] >= (row_first + slot // slots + 1) * tile_size
-
-        @pl.when(uniform)
+        first = n * TOGETHER
+        together = first + TOGETHER <= total
+        for m in range(TOGETHER):
+            together = together & arrive(first + m)
+
+        @pl.when(together)
         def _():
-            step(n, True)
-
-        @pl.when(jnp.logical_not(uniform))
+            for m in range(TOGETHER):
+                step(first + m, True)
+
+        @pl.when(jnp.logical_not(together))
         def _():
-            step(n, False)
+            lax.fori_loop(first, jnp.minimum(first + TOGETHER, total), general, 0)
 
         return carry
 
-    lax.fori_loop(0, total, loop, 0)
+    lax.fori_loop(0, (total + TOGETHER - 1) // TOGETHER, loop, 0)
     multiply(total - 1, 1)
     finish(total - 1)
 
@@ -291,10 +338,10 @@
         pltpu.SMEM((row_tiles * slots + 1,), jnp.int32),
         pltpu.SMEM((rows,), jnp.int32),
         pltpu.SMEM((rows,), jnp.int32),
-        pltpu.VMEM((rows, tile_size, 8 * GROUPS), jnp.bfloat16),
-        pltpu.VMEM((rows, MOMENTS, tile_size), jnp.bfloat16),
+        pltpu.VMEM((rows, 2, tile_size, 8 * GROUPS), jnp.bfloat16),
+        pltpu.VMEM((rows, 2, MOMENTS, tile_size), jnp.bfloat16),
         pltpu.VMEM((2, 8 * GROUPS, tile_size), jnp.bfloat16),
-        pltpu.VMEM((2, MOMENTS, tile_size), jnp.bfloat16),
+        pltpu.VMEM((2, 2, MOMENTS, tile_size), jnp.bfloat16),
         pltpu.VMEM((2, 2, half, tile_size), jnp.bfloat16),
         pltpu.VMEM((2, 2, half, tile_size), jnp.float32),
         pltpu.VMEM((2, MOMENTS, tile_size), jnp.float32),

time: 96.2 us -> 95.3 us (level)
  waiting for transfers between devices: 24.6 us -> 28.6 us
  Pallas kernels: 36.5 us -> 33.7 us
  starting transfers between devices: 31 us -> 28.4 us
    all_to_all x1, waiting for transfers between devices: 8.27 us -> 12.3 us  [body(): lax.all_to_all(col_part.reshape((n_rows,) + local.shape), ROWS, 0, 0, til...]
    all_to_all x1, starting transfers between devices: 9.92 us -> 7.47 us  [body(): lax.all_to_all(col_part.reshape((n_rows,) + local.shape), ROWS, 0, 0, til...]
    pallas_call x1, Pallas kernels: 29.5 us -> 27.2 us  [tile_gradients(): pl.pallas_call(functools.partial(kernel, False), out_shape=[jax.ShapeDtyp...]
where the time goes in v3:
time: 95.3 us; the launch traced here: 94.1 us
  Pallas kernels  33.7 us (35%)
  waiting for transfers between devices  28.6 us (30%)
  starting transfers between devices  28.4 us (30%)
  local copies, waits for them, and re-layouts  3.09 us (3%)
    pallas_call x1, Pallas kernels, tile_gradients(): pl.pallas_call(functools.partial(kernel, False), out_shape=[jax.ShapeDtyp...  27.2 us
    ppermute x3, waiting for transfers between devices, body(): lax.ppermute(local, COLS, [((g + shift) % n_cols, g) for g in range(n_col...  12.3 us
    all_to_all x1, waiting for transfers between devices, body(): lax.all_to_all(col_part.reshape((n_rows,) + local.shape), ROWS, 0, 0, til...  12.3 us
    all_to_all x1, starting transfers between devices, body(): lax.all_to_all(col_pos, ROWS, 0, 0, tiled=True)  9.39 us
    all_to_all x1, starting transfers between devices, body(): lax.all_to_all(col_part.reshape((n_rows,) + local.shape), ROWS, 0, 0, til...  7.47 us
    pallas_call x1, Pallas kernels, own_gradients(): pl.pallas_call(functools.partial(kernel, True), out_shape=jax.ShapeDtypeS...  6.45 us
    ppermute x3, starting transfers between devices, body(): lax.ppermute(local, COLS, [((g + shift) % n_cols, g) for g in range(n_col...  5.93 us
    ppermute x3, starting transfers between devices, body(): lax.ppermute(piece, COLS, [(g, (g + shift) % n_cols) for g in range(n_col...  5.62 us
  transfers between devices with their start and end apart: 8, of which 4 were waited for; matrix products, arithmetic and copies ran while one was open for 0% of the time, Pallas kernels for 7%

profile of v3, /device:TPU:0, one launch (start us, length us, event | category | flops | bytes accessed | tf_op | source)
XLA Modules:
  0.0 94.1 jit_solution(2183412282781529715)
XLA Ops:
  0.0 0.8 reshape.19
  0.9 1.4 %broadcast_in_dim.2 = f32[32,4,24,128]{3,2,1,0:T(8,128)} broadcast(f32[4,24,128]{2,1,0:T(8,128)S(1)} %copy.28.refs_0_), dimensions={1,2,3} | broadcast | bytes 1622016 | tf_op jit(solution)/shard_map/broadcast_in_dim | solution.py:391
  2.2 0.0 copy-start.1
  2.2 0.0 copy-start.2
  2.2 0.0 copy-start
  2.2 9.4 %all-to-all-start = ((f32[32,4,24,128]{3,2,1,0:T(8,128)}), f32[32,4,24,128]{3,2,1,0:T(8,128)S(1)}, u32[]{:S(2)}, u32[]{:S(2)}) async-start(f32[32,4,24,128]{3,2,1,0:T(8,128)} %broadcast_in_dim.2), calls=%async_computation | async-start | bytes 3145728 | tf_op jit(solution)/shard_map/all_to_all | solution.py:392
  11.6 0.1 collective-permute-start.2
  11.7 3.0 %collective-permute-start.1 = (f32[4,24,128]{2,1,0:T(8,128)S(1)}, f32[4,24,128]{2,1,0:T(8,128)S(1)}, u32[]{:S(2)}, u32[]{:S(2)}) collective-permute-start(f32[4,24,128]{2,1,0:T(8,128)S(1)} %copy.28.refs_0_), channel_id=1, source_target_pairs={{2,0},{3,1},{0,2},{1,3},{6,4},{7,5},{4,6},{5,7},{10,8},{11,9},{8,1... | collective-permute-start | bytes 147464 | tf_op jit(solution)/shard_map/ppermute | solution.py:394
  14.7 2.9 %collective-permute-start = (f32[4,24,128]{2,1,0:T(8,128)S(1)}, f32[4,24,128]{2,1,0:T(8,128)S(1)}, u32[]{:S(2)}, u32[]{:S(2)}) collective-permute-start(f32[4,24,128]{2,1,0:T(8,128)S(1)} %copy.28.refs_0_), channel_id=1, source_target_pairs={{1,0},{2,1},{3,2},{0,3},{5,4},{6,5},{7,6},{4,7},{9,8},{10,9},{11,1... | collective-permute-start | bytes 147464 | tf_op jit(solution)/shard_map/ppermute | solution.py:394
  17.6 0.1 pad_add_fusion.group
  17.7 0.0 copy-done.1
  17.7 0.1 copy.30.columns
  17.7 0.0 copy-done.2
  17.7 0.1 copy.31.exponents
  17.8 3.5 %collective-permute-done.2 = f32[4,24,128]{2,1,0:T(8,128)S(1)} collective-permute-done((f32[4,24,128]{2,1,0:T(8,128)S(1)}, f32[4,24,128]{2,1,0:T(8,128)S(1)}, u32[]{:S(2)}, u32[]{:S(2)}) %collective-permute-start.2) | collective-permute-done | bytes 49184 | tf_op jit(solution)/shard_map/ppermute | solution.py:394
  21.3 8.8 %collective-permute-done.1 = f32[4,24,128]{2,1,0:T(8,128)S(1)} collective-permute-done((f32[4,24,128]{2,1,0:T(8,128)S(1)}, f32[4,24,128]{2,1,0:T(8,128)S(1)}, u32[]{:S(2)}, u32[]{:S(2)}) %collective-permute-start.1) | collective-permute-done | bytes 49184 | tf_op jit(solution)/shard_map/ppermute | solution.py:394
  30.2 0.0 collective-permute-done
  30.2 4.0 %all-to-all-done = f32[32,4,24,128]{3,2,1,0:T(8,128)S(1)} async-done(((f32[32,4,24,128]{3,2,1,0:T(8,128)}), f32[32,4,24,128]{3,2,1,0:T(8,128)S(1)}, u32[]{:S(2)}, u32[]{:S(2)}) %all-to-all-start) | async-done | bytes 1572896 | tf_op jit(solution)/shard_map/all_to_all | solution.py:392
  34.1 0.0 copy-done
  34.1 27.2 %tile_gradients.1 = (f32[16,24,128]{2,1,0:T(8,128)S(1)}, f32[128,24,128]{2,1,0:T(8,128)}) custom-call(s32[3]{0:T(128)S(1)} %pad_add_fusion.group, s32[16,2]{1,0:T(8,128)S(1)} %copy.30.columns, s32[16,2]{1,0:T(8,128)S(1)} %copy.31.exponents, s32[24]{0:T(128)S(1)} %copy-done, f32[16,24,128]{2,1,0:T(8,128)S(1)} %pad_maximum_fusion.refs_0_, ...), custom_call_target="tpu_custom_call" | custom-call | tf_op jit(solution)/shard_map/tile_gradients/pallas_call | solution.py:370
  61.4 7.5 %all-to-all-start.1 = ((f32[32,4,24,128]{3,2,1,0:T(8,128)}), f32[32,4,24,128]{3,2,1,0:T(8,128)S(1)}, u32[]{:S(2)}, u32[]{:S(2)}) async-start(f32[32,4,24,128]{3,2,1,0:T(8,128)} %bitcast.5), calls=%async_computation.1 | async-start | bytes 3145728 | tf_op jit(solution)/shard_map/all_to_all | solution.py:400
  68.9 1.3 %collective-permute-start.3 = (f32[4,24,128]{2,1,0:T(8,128)S(1)}, f32[4,24,128]{2,1,0:T(8,128)S(1)}, u32[]{:S(2)}, u32[]{:S(2)}) collective-permute-start(f32[4,24,128]{2,1,0:T(8,128)S(1)} %get-tuple-element.9), channel_id=1, source_target_pairs={{0,1},{1,2},{2,3},{3,0},{4,5},{5,6},{6,7},{7,4},{8,9},{9,10},{10,1... | collective-permute-start | bytes 147464 | tf_op jit(solution)/shard_map/ppermute | solution.py:404
  70.2 2.0 %collective-permute-start.5 = (f32[4,24,128]{2,1,0:T(8,128)S(1)}, f32[4,24,128]{2,1,0:T(8,128)S(1)}, u32[]{:S(2)}, u32[]{:S(2)}) collective-permute-start(f32[4,24,128]{2,1,0:T(8,128)S(1)} %get-tuple-element.10), channel_id=1, source_target_pairs={{0,3},{1,0},{2,1},{3,2},{4,7},{5,4},{6,5},{7,6},{8,11},{9,8},{10,9... | collective-permute-start | bytes 147464 | tf_op jit(solution)/shard_map/ppermute | solution.py:404
  72.2 2.3 %collective-permute-start.4 = (f32[4,24,128]{2,1,0:T(8,128)S(1)}, f32[4,24,128]{2,1,0:T(8,128)S(1)}, u32[]{:S(2)}, u32[]{:S(2)}) collective-permute-start(f32[4,24,128]{2,1,0:T(8,128)S(1)} %get-tuple-element.11), channel_id=1, source_target_pairs={{0,2},{1,3},{2,0},{3,1},{4,6},{5,7},{6,4},{7,5},{8,10},{9,11},{10,... | collective-permute-start | bytes 147464 | tf_op jit(solution)/shard_map/ppermute | solution.py:404
  74.5 6.5 %own_gradients.1 = f32[4,24,128]{2,1,0:T(8,128)S(1)} custom-call(s32[3]{0:T(128)S(1)} %pad_add_fusion.group, s32[16,2]{1,0:T(8,128)S(1)} %copy.30.columns, s32[16,2]{1,0:T(8,128)S(1)} %copy.31.exponents, s32[24]{0:T(128)S(1)} %copy-done, f32[4,24,128]{2,1,0:T(8,128)S(1)} %copy.28.refs_0_, bf16[16,2,512,512]{3,2,1,0:T(8,128)(2,1)} %refs_1_.1), custom_call_target="tpu_custom_call" | custom-call | tf_op jit(solution)/shard_map/own_gradients/pallas_call | solution.py:358
  81.0 12.3 %all-to-all-done.1 = f32[32,4,24,128]{3,2,1,0:T(8,128)S(1)} async-done(((f32[32,4,24,128]{3,2,1,0:T(8,128)}), f32[32,4,24,128]{3,2,1,0:T(8,128)S(1)}, u32[]{:S(2)}, u32[]{:S(2)}) %all-to-all-start.1) | async-done | bytes 1572896 | tf_op jit(solution)/shard_map/all_to_all | solution.py:400
  93.2 0.1 reduce_sum.9
  93.3 0.0 collective-permute-done.3
  93.3 0.0 collective-permute-done.5
  93.4 0.0 collective-permute-done.4
  93.4 0.7 reshape.24
  (7 shorter events, 0.1 us)
Async XLA Ops:
  2.2 15.4 %copy-start.1 = (s32[16,2]{0,1:T(2,128)S(1)}, s32[16,2]{0,1:T(2,128)}, u32[]{:S(2)}) copy-start(s32[16,2]{0,1:T(2,128)} %param.7) | copy-start | bytes 388
  2.2 15.5 %copy-start.2 = (s32[16,2]{0,1:T(2,128)S(1)}, s32[16,2]{0,1:T(2,128)}, u32[]{:S(2)}) copy-start(s32[16,2]{0,1:T(2,128)} %param.8) | copy-start | bytes 388
  2.2 31.9 %copy-start = (s32[24]{0:T(128)S(1)}, s32[24]{0:T(128)}, u32[]{:S(2)}) copy-start(s32[24]{0:T(128)} %starts.3) | copy-start | bytes 292
  2.2 31.9 %all-to-all-start = ((f32[32,4,24,128]{3,2,1,0:T(8,128)}), f32[32,4,24,128]{3,2,1,0:T(8,128)S(1)}, u32[]{:S(2)}, u32[]{:S(2)}) async-start(f32[32,4,24,128]{3,2,1,0:T(8,128)} %broadcast_in_dim.2), calls=%async_computation | async-start | bytes 3145728 | tf_op jit(solution)/shard_map/all_to_all | solution.py:392
  11.6 9.7 %collective-permute-start.2 = (f32[4,24,128]{2,1,0:T(8,128)S(1)}, f32[4,24,128]{2,1,0:T(8,128)S(1)}, u32[]{:S(2)}, u32[]{:S(2)}) collective-permute-start(f32[4,24,128]{2,1,0:T(8,128)S(1)} %copy.28.refs_0_), channel_id=1, source_target_pairs={{3,0},{0,1},{1,2},{2,3},{7,4},{4,5},{5,6},{6,7},{11,8},{8,9},{9,10... | collective-permute-start | bytes 147464 | tf_op jit(solution)/shard_map/ppermute | solution.py:394
  11.7 18.4 %collective-permute-start.1 = (f32[4,24,128]{2,1,0:T(8,128)S(1)}, f32[4,24,128]{2,1,0:T(8,128)S(1)}, u32[]{:S(2)}, u32[]{:S(2)}) collective-permute-start(f32[4,24,128]{2,1,0:T(8,128)S(1)} %copy.28.refs_0_), channel_id=1, source_target_pairs={{2,0},{3,1},{0,2},{1,3},{6,4},{7,5},{4,6},{5,7},{10,8},{11,9},{8,1... | collective-permute-start | bytes 147464 | tf_op jit(solution)/shard_map/ppermute | solution.py:394
  14.7 15.4 %collective-permute-start = (f32[4,24,128]{2,1,0:T(8,128)S(1)}, f32[4,24,128]{2,1,0:T(8,128)S(1)}, u32[]{:S(2)}, u32[]{:S(2)}) collective-permute-start(f32[4,24,128]{2,1,0:T(8,128)S(1)} %copy.28.refs_0_), channel_id=1, source_target_pairs={{1,0},{2,1},{3,2},{0,3},{5,4},{6,5},{7,6},{4,7},{9,8},{10,9},{11,1... | collective-permute-start | bytes 147464 | tf_op jit(solution)/shard_map/ppermute | solution.py:394
  61.4 31.8 %all-to-all-start.1 = ((f32[32,4,24,128]{3,2,1,0:T(8,128)}), f32[32,4,24,128]{3,2,1,0:T(8,128)S(1)}, u32[]{:S(2)}, u32[]{:S(2)}) async-start(f32[32,4,24,128]{3,2,1,0:T(8,128)} %bitcast.5), calls=%async_computation.1 | async-start | bytes 3145728 | tf_op jit(solution)/shard_map/all_to_all | solution.py:400
  68.9 24.4 %collective-permute-start.3 = (f32[4,24,128]{2,1,0:T(8,128)S(1)}, f32[4,24,128]{2,1,0:T(8,128)S(1)}, u32[]{:S(2)}, u32[]{:S(2)}) collective-permute-start(f32[4,24,128]{2,1,0:T(8,128)S(1)} %get-tuple-element.9), channel_id=1, source_target_pairs={{0,1},{1,2},{2,3},{3,0},{4,5},{5,6},{6,7},{7,4},{8,9},{9,10},{10,1... | collective-permute-start | bytes 147464 | tf_op jit(solution)/shard_map/ppermute | solution.py:404
  70.2 23.1 %collective-permute-start.5 = (f32[4,24,128]{2,1,0:T(8,128)S(1)}, f32[4,24,128]{2,1,0:T(8,128)S(1)}, u32[]{:S(2)}, u32[]{:S(2)}) collective-permute-start(f32[4,24,128]{2,1,0:T(8,128)S(1)} %get-tuple-element.10), channel_id=1, source_target_pairs={{0,3},{1,0},{2,1},{3,2},{4,7},{5,4},{6,5},{7,6},{8,11},{9,8},{10,9... | collective-permute-start | bytes 147464 | tf_op jit(solution)/shard_map/ppermute | solution.py:404
  72.2 21.1 %collective-permute-start.4 = (f32[4,24,128]{2,1,0:T(8,128)S(1)}, f32[4,24,128]{2,1,0:T(8,128)S(1)}, u32[]{:S(2)}, u32[]{:S(2)}) collective-permute-start(f32[4,24,128]{2,1,0:T(8,128)S(1)} %get-tuple-element.11), channel_id=1, source_target_pairs={{0,2},{1,3},{2,0},{3,1},{4,6},{5,7},{6,4},{7,5},{8,10},{9,11},{10,... | collective-permute-start | bytes 147464 | tf_op jit(solution)/shard_map/ppermute | solution.py:404
